TPU v7x, 32 devices: a whole 2x2x4 slice. The times are simulated.
32 devices in a mesh: vel: 16 (over z, x, core), box: 2 (over y).
Axes of the slice: x: 2, y: 2, z: 4, core: 2. Of those that a mesh axis runs over, the one named last changes fastest.
Arguments:
- distribution: float32 [4096, 3, 3, 3, 2, 128], P('vel', None, None, None, 'box'), may hold values from -2.5 to 2.5, as said below
- collision_rate: float32 [2, 128], P('box'), may hold values from 1 to 10
Outputs:
- advanced: float32 [4096, 3, 3, 3, 2, 128], P('vel', None, None, None, 'box')
Inputs may be any that keep to these rules, and one draw needn't show every extreme that they name: `distribution`: coefficient (0,0,0) is positive for every box and velocity; every other coefficient is at most coefficient (0,0,0) of the same box and velocity in magnitude.
All inputs are finite; a program needn't handle non-finite values.
Results may differ from a plain program's by a relative error of at most 0.0003.
Values sent between devices are 32-bit elements; how exact they have to be, the bound alone decides.
A program may use at most 64 MiB of HBM per device.

v0:
```python
import jax
import jax.numpy as jnp
from jax import lax
from jax.sharding import PartitionSpec as P

VPD = 16
NZ = 16


SPEED_LIMIT = 4.0
TIME_STEP = 0.02
HIGHEST = lax.Precision.HIGHEST


def passed_along(block, axis, distance):
    devices = range(lax.axis_size(axis))
    route = [((i - distance) % len(devices), i) for i in devices]
    return lax.ppermute(block, axis, route)


def speeds(index):
    spacing = 2.0 * SPEED_LIMIT / VPD
    first = index // (VPD * VPD)
    second = index // VPD % VPD
    third = index % VPD

    def centre(number):
        return -SPEED_LIMIT + (number.astype(jnp.float32) + 0.5) * spacing

    return (centre(first), centre(second), centre(third))


def moment_table(index):
    speed_x, speed_y, speed_z = speeds(index)
    weight = (2.0 * SPEED_LIMIT / VPD) ** 3
    energy = 0.5 * (speed_x * speed_x + speed_y * speed_y + speed_z * speed_z)
    return weight * jnp.stack([jnp.ones_like(speed_x), speed_x, speed_y, speed_z, energy])


def primitives(totals):
    density = totals[0]
    flow = totals[1:4] / density
    temper = (2.0 * totals[4] / density - jnp.sum(flow * flow, axis=0)) / 3.0
    return jnp.concatenate([density[None], flow, temper[None]], axis=0)


def face_traces(field, axis):
    first = jnp.take(field, 0, axis)
    second = jnp.take(field, 1, axis)
    third = jnp.take(field, 2, axis)
    return (first + second + third, first - second + third)


def transport(field, axis, speed, upper, lower, upper_prev, lower_next):
    positive = speed > 0
    upper_flux = jnp.where(positive, upper, lower_next)
    lower_flux = jnp.where(positive, upper_prev, lower)
    first = jnp.take(field, 0, axis)
    second = jnp.take(field, 1, axis)
    rate_zero = speed * (lower_flux - upper_flux)
    rate_one = 3.0 * speed * (2.0 * first - upper_flux - lower_flux)
    rate_two = 5.0 * speed * (2.0 * second - upper_flux + lower_flux)
    return jnp.stack([rate_zero, rate_one, rate_two], axis)


def z_previous(values):
    cells = jnp.arange(values.shape[-1], dtype=jnp.int32) % NZ
    return jnp.where(cells == 0, jnp.roll(values, 1 - NZ, -1), jnp.roll(values, 1, -1))


def z_following(values):
    cells = jnp.arange(values.shape[-1], dtype=jnp.int32) % NZ
    return jnp.where(cells == NZ - 1, jnp.roll(values, NZ - 1, -1), jnp.roll(values, -1, -1))


def block_rate(field, index, states, collision_rate, upper_prev, lower_next):
    speed_x, speed_y, speed_z = speeds(index)
    shaped = (-1, 1, 1, 1, 1)
    upper, lower = face_traces(field, 1)
    total = transport(field, 1, speed_x.reshape(shaped), upper, lower, upper_prev, lower_next)
    upper, lower = face_traces(field, 2)
    total = total + transport(
        field,
        2,
        speed_y.reshape(shaped),
        upper,
        lower,
        jnp.roll(upper, NZ, -1),
        jnp.roll(lower, -NZ, -1),
    )
    upper, lower = face_traces(field, 3)
    total = total + transport(
        field, 3, speed_z.reshape(shaped), upper, lower, z_previous(upper), z_following(lower)
    )
    density = states[0]
    temper = states[4]
    offset_x = speed_x[:, None, None] - states[1]
    offset_y = speed_y[:, None, None] - states[2]
    offset_z = speed_z[:, None, None] - states[3]
    spread = offset_x * offset_x + offset_y * offset_y + offset_z * offset_z
    maxwell = density * (2.0 * jnp.pi * temper) ** (-1.5) * jnp.exp(-spread / (2.0 * temper))
    total = total - collision_rate * field
    return total.at[:, 0, 0, 0].add(collision_rate * maxwell)


def shards(distribution, collision_rate):
    count = distribution.shape[0]
    index = lax.axis_index("vel") * count + jnp.arange(count, dtype=jnp.int32)
    table = moment_table(index)

    def section_rate(field):
        base = field[:, 0, 0, 0].reshape(count, -1)
        partial_terms = jnp.dot(table, base, precision=HIGHEST)
        totals = lax.psum(partial_terms, "vel")
        states = primitives(totals)
        states = states.reshape((5,) + field.shape[4:])
        upper, lower = face_traces(field, 1)
        from_left = passed_along(upper, "box", 1)
        from_right = passed_along(lower, "box", -1)
        upper_prev = jnp.concatenate([from_left, upper[:, :, :, :-1]], axis=3)
        lower_next = jnp.concatenate([lower[:, :, :, 1:], from_right], axis=3)
        return block_rate(field, index, states, collision_rate, upper_prev, lower_next)

    middle = distribution + TIME_STEP * section_rate(distribution)
    final_rate = section_rate(middle)
    return 0.5 * distribution + 0.5 * (middle + TIME_STEP * final_rate)


def solution(mesh):
    return jax.shard_map(
        shards,
        mesh=mesh,
        in_specs=(P("vel", None, None, None, "box", None), P("box", None)),
        out_specs=P("vel", None, None, None, "box", None),
        check_vma=False,
    )
```

profile of v0, /device:TPU:0, one launch (start us, length us, event | category | flops | bytes accessed | tf_op | source)
XLA Modules:
  0.0 183.4 jit_solution(10867688493453165227)
XLA Ops:
  0.0 2.4 %copy.88 = f32[256,3,3,3,1,128]{5,0,3,2,4,1:T(8,128)S(1)} copy(f32[256,3,3,3,1,128]{5,4,3,2,1,0:T(1,128)} %param.24) | data formatting | bytes 7077888 | tf_op args[0]
  2.4 1.3 fusion.45
  3.8 3.0 %collective-permute-start.1 = (f32[256,3,3,1,128]{4,0,3,2,1:T(8,128)}, f32[256,3,3,1,128]{4,0,3,2,1:T(8,128)}, u32[]{:S(2)}, u32[]{:S(2)}) collective-permute-start(f32[256,3,3,1,128]{4,0,3,2,1:T(8,128)} %fusion.45), channel_id=1, source_target_pairs={{1,0},{0,1},{3,2},{2,3},{5,4},{4,5},{7,6},{6,7},{9,8},{8,9},{11,10... | collective-permute-start | bytes 3538952 | tf_op jit(solution)/shard_map/ppermute | solution.py:18
  6.7 1.2 bitcast_add_fusion
  7.9 0.8 collective-permute-start
  14.3 3.5 %fusion.50 = (f32[256,3,1,3,1,128]{5,4,3,2,1,0:T(1,128)}, f32[256,3,1,3,1,128]{5,4,3,2,1,0:T(1,128)}, f32[256,3,1,3,1,128]{5,4,3,2,1,0:T(1,128)}) fusion(f32[256,3,3,3,1,128]{5,4,3,2,1,0:T(1,128)S(1)} %copy-done), kind=kLoop, calls=%fused_computation.176 | loop fusion | bytes 7077888 | tf_op jit(solution)/shard_map/jit(_take) | solution.py:49
  17.8 3.5 %fusion.51 = (f32[256,3,3,1,1,128]{5,4,3,2,1,0:T(1,128)}, f32[256,3,3,1,1,128]{5,4,3,2,1,0:T(1,128)}, f32[256,3,3,1,1,128]{5,4,3,2,1,0:T(1,128)}) fusion(f32[256,3,3,3,1,128]{5,4,3,2,1,0:T(1,128)S(1)} %copy-done), kind=kLoop, calls=%fused_computation.177 | loop fusion | bytes 7077888 | tf_op jit(solution)/shard_map/jit(_take) | solution.py:49
  22.5 1.7 fusion.18
  24.2 34.0 %psum.14 = f32[5,128]{1,0:T(8,128)} all-reduce(f32[5,128]{1,0:T(8,128)} %fusion.18), channel_id=1, replica_groups=mesh['vel'=16,'box'=2] {'vel'}, use_global_device_ids=true, to_apply=%region_0.10 | all-reduce | flops 640 | bytes 5120 | tf_op jit(solution)/shard_map/psum | solution.py:114
  59.6 0.8 multiply_bitcast_fusion.18
  60.4 2.2 %subtract_add_fusion.4 = (f32[256,3,3,1,128]{4,0,2,1,3:T(8,128)S(1)}, f32[256,3,3,1,128]{4,0,2,1,3:T(8,128)S(1)}) fusion(f32[256,3,1,3,1,128]{5,4,3,2,1,0:T(1,128)} %get-tuple-element.182, f32[256,3,1,3,1,128]{5,4,3,2,1,0:T(1,128)} %get-tuple-element.183, f32[256,3,1,3,1,128]{5,4,3,2,1,0:T(1,128)} %get-tuple-element.181), kind=kLoop, calls=%fused_computation.78 | loop fusion | flops 1179648 | bytes 5898240 | tf_op jit(solution)/shard_map/add | solution.py:51
  65.4 0.8 multiply_bitcast_fusion.14
  68.1 1.4 multiply_bitcast_fusion.11
  70.9 1.5 copy-done.4
  72.3 2.1 %fusion.10 = (f32[256,1,3,3,1,128]{5,0,3,2,4,1:T(8,128)S(1)}, f32[256,3,3,1,128]{4,0,2,1,3:T(8,128)S(1)}) fusion(f32[256,3,3,1,128]{4,0,3,2,1:T(8,128)} %collective-permute-done.1, f32[256]{0:T(256)S(1)} %copy-done.15, pred[256]{0:T(512)(128)(4,1)S(1)} %broadcast_compare_fusion.2, f32[256,3,3,3,1,128]{5,0,3,2,4,1:T(8,128)S(1)} %copy-done.4, ...), kind=kLoop, calls=%fused_computation.49 | loop fusion | flops 2359296 | bytes 8258816 | tf_op jit(solution)/shard_map/stack | solution.py:63
  74.5 1.8 fusion.13
  76.3 1.8 fusion.8
  78.2 1.4 fusion.1
  80.7 0.8 fusion.14
  81.5 2.4 %subtract_add_fusion.1 = (f32[256,3,3,1,128]{4,0,2,1,3:T(8,128)}, f32[256,3,3,1,128]{4,0,3,2,1:T(8,128)}, f32[256,3,3,1,128]{4,0,2,1,3:T(8,128)}, f32[256,3,3,1,128]{4,0,3,2,1:T(8,128)}) fusion(f32[256,3,3,3,1,128]{5,0,3,2,4,1:T(8,128)S(1)} %multiply_add_fusion), kind=kLoop, calls=%fused_computation.63 | loop fusion | flops 2359296 | bytes 11796480 | tf_op jit(solution)/shard_map/add | solution.py:51
  83.9 29.7 %psum.15 = f32[5,128]{1,0:T(8,128)S(1)} all-reduce(f32[5,128]{1,0:T(8,128)S(1)} %copy-done.14), channel_id=1, replica_groups=mesh['vel'=16,'box'=2] {'vel'}, use_global_device_ids=true, to_apply=%region_2.12 | all-reduce | flops 640 | bytes 5120 | tf_op jit(solution)/shard_map/psum | solution.py:114
  113.7 1.8 slice.477
  115.9 1.0 collective-permute-start.3
  116.9 1.1 collective-permute-start.2
  118.8 25.9 %collective-permute-done.3 = f32[256,3,3,1,128]{4,0,3,2,1:T(8,128)S(1)} collective-permute-done((f32[256,3,3,1,128]{4,0,3,2,1:T(8,128)S(1)}, f32[256,3,3,1,128]{4,0,3,2,1:T(8,128)S(1)}, u32[]{:S(2)}, u32[]{:S(2)}) %collective-permute-start.3) | collective-permute-done | bytes 1179680 | tf_op jit(solution)/shard_map/ppermute | solution.py:18
  144.8 24.2 %collective-permute-done.2 = f32[256,3,3,1,128]{4,0,3,2,1:T(8,128)S(1)} collective-permute-done((f32[256,3,3,1,128]{4,0,3,2,1:T(8,128)S(1)}, f32[256,3,3,1,128]{4,0,3,2,1:T(8,128)S(1)}, u32[]{:S(2)}, u32[]{:S(2)}) %collective-permute-start.2) | collective-permute-done | bytes 1179680 | tf_op jit(solution)/shard_map/ppermute | solution.py:18
  169.0 1.7 multiply_bitcast_fusion.4
  172.5 1.4 multiply_bitcast_fusion.2
  173.9 1.0 multiply_bitcast_fusion.7
  175.0 1.6 fusion.2
  177.0 1.0 add_multiply_fusion
  178.0 5.4 %copy.89 = f32[256,3,3,3,1,128]{5,4,3,2,1,0:T(1,128)} copy(f32[256,3,3,3,1,128]{5,0,3,2,4,1:T(8,128)S(1)} %add_multiply_fusion) | data formatting | bytes 7077888 | tf_op jit(solution)/shard_map/add | solution.py:126
  (123 shorter events, 18.6 us)
Async XLA Ops:
  2.4 4.3 %copy-start.3 = (f32[256,3,3,3,1,128]{5,0,3,2,4,1:T(8,128)}, f32[256,3,3,3,1,128]{5,0,3,2,4,1:T(8,128)S(1)}, u32[]{:S(2)}) copy-start(f32[256,3,3,3,1,128]{5,0,3,2,4,1:T(8,128)S(1)} %copy.88) | copy-start | bytes 10616836
  3.8 9.8 %copy-start = (f32[256,3,3,3,1,128]{5,4,3,2,1,0:T(1,128)S(1)}, f32[256,3,3,3,1,128]{5,4,3,2,1,0:T(1,128)}, u32[]{:S(2)}) copy-start(f32[256,3,3,3,1,128]{5,4,3,2,1,0:T(1,128)} %param.24) | copy-start | bytes 10616836
  3.8 67.1 %collective-permute-start.1 = (f32[256,3,3,1,128]{4,0,3,2,1:T(8,128)}, f32[256,3,3,1,128]{4,0,3,2,1:T(8,128)}, u32[]{:S(2)}, u32[]{:S(2)}) collective-permute-start(f32[256,3,3,1,128]{4,0,3,2,1:T(8,128)} %fusion.45), channel_id=1, source_target_pairs={{1,0},{0,1},{3,2},{2,3},{5,4},{4,5},{7,6},{6,7},{9,8},{8,9},{11,10... | collective-permute-start | bytes 3538952 | tf_op jit(solution)/shard_map/ppermute | solution.py:18
  7.9 62.9 %collective-permute-start = (f32[256,3,3,1,128]{4,0,3,2,1:T(8,128)}, f32[256,3,3,1,128]{4,0,3,2,1:T(8,128)}, u32[]{:S(2)}, u32[]{:S(2)}) collective-permute-start(f32[256,3,3,1,128]{4,0,3,2,1:T(8,128)} %bitcast_add_fusion), channel_id=1, source_target_pairs={{1,0},{0,1},{3,2},{2,3},{5,4},{4,5},{7,6},{6,7},{9,8},{8,9},{11,10... | collective-permute-start | bytes 3538952 | tf_op jit(solution)/shard_map/ppermute | solution.py:18
  63.0 1.7 copy-start.8
  66.2 10.1 %copy-start.31 = (pred[256]{0:T(512)(128)(4,1)}, pred[256]{0:T(512)(128)(4,1)S(1)}, u32[]{:S(2)}) copy-start(pred[256]{0:T(512)(128)(4,1)S(1)} %broadcast_compare_fusion.2) | copy-start | bytes 772
  68.1 1.4 copy-start.9
  68.1 1.6 copy-start.10
  68.1 1.6 copy-start.25
  68.1 1.6 copy-start.27
  70.3 2.0 %copy-start.4 = (f32[256,3,3,3,1,128]{5,0,3,2,4,1:T(8,128)S(1)}, f32[256,3,3,3,1,128]{5,0,3,2,4,1:T(8,128)}, u32[]{:S(2)}) copy-start(f32[256,3,3,3,1,128]{5,0,3,2,4,1:T(8,128)} %copy-done.3) | copy-start | bytes 10616836
  70.3 2.0 %copy-start.15 = (f32[256]{0:T(256)S(1)}, f32[256]{0:T(256)}, u32[]{:S(2)}) copy-start(f32[256]{0:T(256)} %multiply_add_fusion.3) | copy-start | bytes 3076
  70.8 3.7 %copy-start.23 = (f32[256]{0:T(256)S(1)}, f32[256]{0:T(256)}, u32[]{:S(2)}) copy-start(f32[256]{0:T(256)} %get-tuple-element.208) | copy-start | bytes 3076
  74.5 1.8 copy-start.21
  76.3 1.8 %copy-start.29 = (f32[1,128]{1,0:T(1,128)S(1)}, f32[1,128]{1,0:T(1,128)}, u32[]{:S(2)}) copy-start(f32[1,128]{1,0:T(1,128)} %param.25) | copy-start | bytes 1540
  78.2 2.0 %copy-start.1 = (f32[256,3,3,3,1,128]{5,4,3,2,1,0:T(1,128)S(1)}, f32[256,3,3,3,1,128]{5,4,3,2,1,0:T(1,128)}, u32[]{:S(2)}) copy-start(f32[256,3,3,3,1,128]{5,4,3,2,1,0:T(1,128)} %param.24) | copy-start | bytes 10616836
  81.5 2.4 %copy-start.14 = (f32[5,128]{1,0:T(8,128)S(1)}, f32[5,128]{1,0:T(8,128)}, u32[]{:S(2)}) copy-start(f32[5,128]{1,0:T(8,128)} %fusion.14) | copy-start | bytes 7684
  113.6 1.8 copy-start.6
  113.7 2.2 %copy-start.13 = (f32[256,3,3,1,128]{4,0,3,2,1:T(8,128)S(1)}, f32[256,3,3,1,128]{4,0,3,2,1:T(8,128)}, u32[]{:S(2)}) copy-start(f32[256,3,3,1,128]{4,0,3,2,1:T(8,128)} %get-tuple-element.174) | copy-start | bytes 3538948
  115.5 1.4 copy-start.12
  115.5 2.6 %copy-start.5 = (f32[256,3,3,1,128]{4,0,2,1,3:T(8,128)S(1)}, f32[256,3,3,1,128]{4,0,2,1,3:T(8,128)}, u32[]{:S(2)}) copy-start(f32[256,3,3,1,128]{4,0,2,1,3:T(8,128)} %get-tuple-element.173) | copy-start | bytes 3538948
  115.5 2.6 %copy-start.40 = (pred[256]{0:T(512)(128)(4,1)S(1)}, pred[256]{0:T(512)(128)(4,1)}, u32[]{:S(2)}) copy-start(pred[256]{0:T(512)(128)(4,1)} %get-tuple-element.212) | copy-start | bytes 772
  115.9 28.9 %collective-permute-start.3 = (f32[256,3,3,1,128]{4,0,3,2,1:T(8,128)S(1)}, f32[256,3,3,1,128]{4,0,3,2,1:T(8,128)S(1)}, u32[]{:S(2)}, u32[]{:S(2)}) collective-permute-start(f32[256,3,3,1,128]{4,0,3,2,1:T(8,128)S(1)} %copy-done.13), channel_id=1, source_target_pairs={{1,0},{0,1},{3,2},{2,3},{5,4},{4,5},{7,6},{6,7},{9,8},{8,9},{11,10... | collective-permute-start | bytes 3538952 | tf_op jit(solution)/shard_map/ppermute | solution.py:18
  116.9 52.1 %collective-permute-start.2 = (f32[256,3,3,1,128]{4,0,3,2,1:T(8,128)S(1)}, f32[256,3,3,1,128]{4,0,3,2,1:T(8,128)S(1)}, u32[]{:S(2)}, u32[]{:S(2)}) collective-permute-start(f32[256,3,3,1,128]{4,0,3,2,1:T(8,128)S(1)} %copy-done.12), channel_id=1, source_target_pairs={{1,0},{0,1},{3,2},{2,3},{5,4},{4,5},{7,6},{6,7},{9,8},{8,9},{11,10... | collective-permute-start | bytes 3538952 | tf_op jit(solution)/shard_map/ppermute | solution.py:18
  118.0 50.9 %copy-start.16 = (f32[256]{0:T(256)S(1)}, f32[256]{0:T(256)}, u32[]{:S(2)}) copy-start(f32[256]{0:T(256)} %multiply_add_fusion.3) | copy-start | bytes 3076
  118.1 50.9 %copy-start.26 = (f32[256]{0:T(256)S(1)}, f32[256]{0:T(256)}, u32[]{:S(2)}) copy-start(f32[256]{0:T(256)} %get-tuple-element.206) | copy-start | bytes 3076
  118.1 50.9 %copy-start.28 = (f32[256]{0:T(256)S(1)}, f32[256]{0:T(256)}, u32[]{:S(2)}) copy-start(f32[256]{0:T(256)} %get-tuple-element.210) | copy-start | bytes 3076
  118.1 50.9 %copy-start.32 = (pred[256]{0:T(512)(128)(4,1)S(1)}, pred[256]{0:T(512)(128)(4,1)}, u32[]{:S(2)}) copy-start(pred[256]{0:T(512)(128)(4,1)} %copy-done.31) | copy-start | bytes 772
  172.5 1.4 copy-start.20
  172.5 1.4 copy-start.22
  172.5 1.4 copy-start.24
  175.0 2.0 %copy-start.2 = (f32[256,3,3,3,1,128]{5,4,3,2,1,0:T(1,128)S(1)}, f32[256,3,3,3,1,128]{5,4,3,2,1,0:T(1,128)}, u32[]{:S(2)}) copy-start(f32[256,3,3,3,1,128]{5,4,3,2,1,0:T(1,128)} %param.24) | copy-start | bytes 10616836
  (13 other events, 10.9 us)
where the time goes:
time: 184 us; the launch traced here: 183 us
  blocking collectives  63.7 us (35%)
  waiting for transfers between devices  50.1 us (27%)
  other arithmetic  32.7 us (18%)
  local copies, waits for them, and re-layouts  28 us (15%)
  starting transfers between devices  5.89 us (3%)
  matrix products  2.45 us (1%)
    psum x2, blocking collectives, section_rate(): totals = lax.psum(partial_terms, 'vel')  63.7 us
    ppermute x4, waiting for transfers between devices, passed_along(): return lax.ppermute(block, axis, route)  50.1 us
    another operation x11, other arithmetic, transport(): return jnp.stack([rate_zero, rate_one, rate_two], axis)  13.8 us
    add x5, other arithmetic, face_traces(): return (first + second + third, first - second + third)  7.52 us
    unnamed x83, local copies, waits for them, and re-layouts  7.09 us
    another operation x2, local copies, waits for them, and re-layouts, face_traces(): second = jnp.take(field, 1, axis)  6.92 us
    ppermute x4, starting transfers between devices, passed_along(): return lax.ppermute(block, axis, route)  5.89 us
    add x1, local copies, waits for them, and re-layouts, shards(): return 0.5 * distribution + 0.5 * (middle + TIME_STEP * final_rate)  5.43 us
  transfers between devices with their start and end apart: 4, of which 2 were waited for; matrix products, arithmetic and copies ran while one was open for 15% of the time, Pallas kernels for 0%

commit v1 on v0

v1 whole, which is shorter than its diff:
```python
import functools

import jax
import jax.numpy as jnp
from jax import lax
from jax.experimental import pallas as pl
from jax.experimental.pallas import tpu as pltpu
from jax.sharding import PartitionSpec as P

VPD = 16
NZ = 16
MODES = 3

SPEED_LIMIT = 4.0
TIME_STEP = 0.02
SPACING = 2.0 * SPEED_LIMIT / VPD
CUBE = MODES ** 3
FACE = MODES ** 2
SUB = 8
HALVES = VPD // SUB
MESH = pl.DeviceIdType.MESH


def centre(number):
    return -SPEED_LIMIT + (number.astype(jnp.float32) + 0.5) * SPACING


def line_modes(dim, number):
    stride = MODES ** (2 - dim)
    first = number // stride * stride * MODES + number % stride
    return [first + a * stride for a in range(MODES)]


def kernel(nvel, nbox, count, f_hbm, nu_ref, out_hbm, f_v, o_v, mid, trace, halo,
           slots, in_sem, out_sem, x_send, x_recv, m_send, m_recv):
    lanes = f_v.shape[-1]
    chunks = count // VPD
    rows = VPD * CUBE
    me_vel = lax.axis_index("vel")
    me_box = lax.axis_index("box")
    start = me_vel * count
    first = start // (VPD * VPD)
    positive = first >= VPD // 2
    ahead = lax.rem(me_box + 1, nbox)
    behind = lax.rem(me_box + nbox - 1, nbox)
    target = jnp.where(positive, ahead, behind)
    source = jnp.where(positive, behind, ahead)

    def load_copy(c):
        part = pl.ds(pl.multiple_of(c * rows, SUB), rows)
        return pltpu.make_async_copy(f_hbm.at[part], f_v.at[part], in_sem.at[c])

    def store_copy(c):
        part = pl.ds(pl.multiple_of(c * rows, SUB), rows)
        return pltpu.make_async_copy(o_v.at[part], out_hbm.at[part], out_sem.at[c])

    def halo_copy(section, c):
        return pltpu.make_async_remote_copy(
            src_ref=trace.at[section, c], dst_ref=halo.at[section, c],
            send_sem=x_send.at[section, c], recv_sem=x_recv.at[section, c],
            device_id={"box": target}, device_id_type=MESH)

    def moment_copy(section, k, slot):
        return pltpu.make_async_remote_copy(
            src_ref=slots.at[section, slot], dst_ref=slots.at[section, slot],
            send_sem=m_send.at[section, k], recv_sem=m_recv.at[section, slot],
            device_id={"vel": lax.rem(me_vel + k, nvel)}, device_id_type=MESH)

    def each(low, high, body):
        def step(i, carry):
            body(i)
            return carry
        lax.fori_loop(low, high, step, 0)

    each(0, chunks, lambda c: load_copy(c).start())

    barrier = pltpu.get_barrier_semaphore()
    pl.semaphore_signal(barrier, inc=1, device_id={"box": source}, device_id_type=MESH)
    each(1, nvel, lambda k: pl.semaphore_signal(
        barrier, inc=1, device_id={"vel": lax.rem(me_vel + k, nvel)}, device_id_type=MESH))
    pl.semaphore_wait(barrier, nvel)

    speed_x = centre(first)
    sign_x = jnp.where(positive, 1.0, -1.0)
    row = lax.broadcasted_iota(jnp.int32, (SUB, lanes), 0)
    cell = lax.broadcasted_iota(jnp.int32, (SUB, lanes), 1) % NZ
    speeds_z = [centre(row + h * SUB) for h in range(HALVES)]

    def z_neighbour(values, h):
        if 2 * h >= HALVES:
            return jnp.where(cell == 0, pltpu.roll(values, lanes + 1 - NZ, 1), pltpu.roll(values, 1, 1))
        return jnp.where(cell == NZ - 1, pltpu.roll(values, NZ - 1, 1), pltpu.roll(values, lanes - 1, 1))

    def field(c, h):
        base = (c * VPD + h * SUB) * CUBE
        return [f_v[pl.ds(base + m, SUB, stride=CUBE), :] for m in range(CUBE)]

    def put_trace(section, c, h, values):
        for q in range(FACE):
            m0, m1, m2 = (values[m] for m in line_modes(0, q))
            trace[section, c, h * FACE + q] = m0 + m2 + sign_x * m1

    def gathered(sums, c, h, base):
        speed_y = centre(lax.rem(start // VPD + c, VPD))
        speed_z = speeds_z[h]
        zero, along_y, along_z, square = sums
        return (zero + base, along_y + speed_y * base, along_z + speed_z * base,
                square + (speed_y * speed_y + speed_z * speed_z) * base)

    def exchange(section, sums):
        zero, along_y, along_z, square = (jnp.sum(s, axis=0, keepdims=True) for s in sums)
        weight = SPACING ** 3
        terms = (zero, speed_x * zero, along_y, along_z, 0.5 * (speed_x * speed_x * zero + square))
        tile = jnp.zeros((SUB, lanes), jnp.float32)
        for r, term in enumerate(terms):
            tile = jnp.where(row == r, weight * term, tile)
        slots[section, me_vel] = tile
        each(1, nvel, lambda k: moment_copy(section, k, me_vel).start())

    def states(section):
        each(1, nvel, lambda k: moment_copy(section, k, lax.rem(me_vel + k, nvel)).wait_recv())
        total = lax.fori_loop(1, nvel, lambda k, s: s + slots[section, k], slots[section, 0])
        density = total[0:1]
        flow = [total[r:r + 1] / density for r in (1, 2, 3)]
        square = flow[0] * flow[0] + flow[1] * flow[1] + flow[2] * flow[2]
        temper = (2.0 * total[4:5] / density - square) / 3.0
        root = 1.0 / jnp.sqrt(2.0 * jnp.pi * temper)
        nu = TIME_STEP * nu_ref[...]
        wide = lambda v: jnp.broadcast_to(v, (SUB, lanes))
        return (wide(nu * density * (root * root * root)), wide(flow[0]), wide(flow[1]), wide(flow[2]),
                wide(-0.5 / temper))

    keep = jnp.broadcast_to(1.0 - TIME_STEP * nu_ref[...], (SUB, lanes))

    def stepped(section, c, h, m, state):
        second = lax.rem(start // VPD + c, VPD)
        speed_y = centre(second)
        up_y = second >= VPD // 2
        sign_y = jnp.where(up_y, 1.0, -1.0)
        shift_y = jnp.where(up_y, NZ, lanes - NZ)
        speed_z = speeds_z[h]
        up_z = 2 * h >= HALVES
        acc = [keep * v for v in m]

        def transport(dim, speed, size, own, other):
            a = TIME_STEP * size
            w3 = (3.0 * TIME_STEP) * speed
            w10 = (10.0 * TIME_STEP) * speed
            for q in range(FACE):
                i0, i1, i2 = line_modes(dim, q)
                mine = own(q, i0, i1, i2)
                near = other(q, mine)
                jump = a * (near - mine)
                acc[i0] = acc[i0] + jump
                acc[i1] = acc[i1] + w3 * ((m[i0] + m[i0]) - (mine + near))
                acc[i2] = acc[i2] + (w10 * m[i1] + 5.0 * jump)

        transport(2, speed_z, speed_z if up_z else -speed_z,
                  lambda q, i0, i1, i2: m[i0] + m[i2] + m[i1] if up_z else m[i0] + m[i2] - m[i1],
                  lambda q, mine: z_neighbour(mine, h))
        transport(1, speed_y, sign_y * speed_y,
                  lambda q, i0, i1, i2: m[i0] + m[i2] + sign_y * m[i1],
                  lambda q, mine: pltpu.roll(mine, shift_y, 1))
        transport(0, speed_x, sign_x * speed_x,
                  lambda q, i0, i1, i2: trace[section, c, h * FACE + q],
                  lambda q, mine: halo[section, c, h * FACE + q])
        scale, flow_x, flow_y, flow_z, narrow = state
        off_x = speed_x - flow_x
        off_y = speed_y - flow_y
        off_z = speed_z - flow_z
        spread = off_x * off_x + off_y * off_y + off_z * off_z
        acc[0] = acc[0] + scale * jnp.exp(spread * narrow)
        return acc

    zeros = (jnp.zeros((SUB, lanes), jnp.float32),) * 4

    def opening(c, sums):
        load_copy(c).wait()
        for h in range(HALVES):
            values = field(c, h)
            put_trace(0, c, h, values)
            sums = gathered(sums, c, h, values[0])
        halo_copy(0, c).start()
        return sums

    exchange(0, lax.fori_loop(0, chunks, opening, zeros))
    state_one = states(0)

    def section_one(c, sums):
        halo_copy(0, c).wait_recv()
        for h in range(HALVES):
            acc = stepped(0, c, h, field(c, h), state_one)
            for m in range(CUBE):
                mid[c * HALVES + h, m] = acc[m]
            put_trace(1, c, h, acc)
            sums = gathered(sums, c, h, acc[0])
        halo_copy(1, c).start()
        return sums

    exchange(1, lax.fori_loop(0, chunks, section_one, zeros))
    state_two = states(1)

    def section_two(c):
        halo_copy(1, c).wait_recv()
        for h in range(HALVES):
            values = [mid[c * HALVES + h, m] for m in range(CUBE)]
            acc = stepped(1, c, h, values, state_two)
            base = (c * VPD + h * SUB) * CUBE
            for m in range(CUBE):
                place = pl.ds(base + m, SUB, stride=CUBE)
                o_v[place, :] = 0.5 * f_v[place, :] + 0.5 * acc[m]
        store_copy(c).start()

    each(0, chunks, section_two)

    for section in range(2):
        each(0, chunks, lambda c: halo_copy(section, c).wait_send())
        each(1, nvel, lambda k: moment_copy(section, k, me_vel).wait_send())
    each(0, chunks, lambda c: store_copy(c).wait())


def shards(nvel, nbox, distribution, collision_rate):
    count = distribution.shape[0]
    lanes = distribution.shape[-1]
    assert (VPD * VPD) % count == 0 and count % VPD == 0
    assert distribution.shape[4] == 1
    chunks = count // VPD
    total = count * CUBE
    f32 = jnp.float32
    out = pl.pallas_call(
        functools.partial(kernel, nvel, nbox, count),
        out_shape=jax.ShapeDtypeStruct((total, lanes), f32),
        in_specs=[pl.BlockSpec(memory_space=pl.ANY), pl.BlockSpec(memory_space=pltpu.VMEM)],
        out_specs=pl.BlockSpec(memory_space=pl.ANY),
        scratch_shapes=[
            pltpu.VMEM((total, lanes), f32),
            pltpu.VMEM((total, lanes), f32),
            pltpu.VMEM((chunks * HALVES, CUBE, SUB, lanes), f32),
            pltpu.VMEM((2, chunks, HALVES * FACE, SUB, lanes), f32),
            pltpu.VMEM((2, chunks, HALVES * FACE, SUB, lanes), f32),
            pltpu.VMEM((2, nvel, SUB, lanes), f32),
            pltpu.SemaphoreType.DMA((chunks,)),
            pltpu.SemaphoreType.DMA((chunks,)),
            pltpu.SemaphoreType.DMA((2, chunks)),
            pltpu.SemaphoreType.DMA((2, chunks)),
            pltpu.SemaphoreType.DMA((2, nvel)),
            pltpu.SemaphoreType.DMA((2, nvel)),
        ],
        compiler_params=pltpu.CompilerParams(
            collective_id=0, has_side_effects=True, vmem_limit_bytes=40 * 2 ** 20),
        cost_estimate=pl.CostEstimate(flops=total * lanes * 80, bytes_accessed=total * lanes * 8,
                                      transcendentals=2 * count * lanes),
    )(distribution.reshape(total, lanes), collision_rate)
    return out.reshape(distribution.shape)


def solution(mesh):
    return jax.shard_map(
        functools.partial(shards, mesh.shape["vel"], mesh.shape["box"]),
        mesh=mesh,
        in_specs=(P("vel", None, None, None, "box", None), P("box", None)),
        out_specs=P("vel", None, None, None, "box", None),
        check_vma=False,
    )
```

time: 184 us -> 70.8 us (0.38)
  Pallas kernels: 0 us -> 66.1 us
  blocking collectives: 63.7 us -> 0 us
  waiting for transfers between devices: 50.1 us -> 0 us
  other arithmetic: 32.7 us -> 0 us
  local copies, waits for them, and re-layouts: 28 us -> 4.45 us
  starting transfers between devices: 5.89 us -> 0 us
  matrix products: 2.45 us -> 0 us
    pallas_call x0 -> x1, Pallas kernels: none -> 66.1 us  [shards(): pl.pallas_call(functools.partial(kernel, nvel, nbox, count), out_shape=ja...]
    psum x2 -> x0, blocking collectives: 63.7 us -> none  [section_rate(): totals = lax.psum(partial_terms, 'vel')]
    ppermute x4 -> x0, waiting for transfers between devices: 50.1 us -> none  [passed_along(): return lax.ppermute(block, axis, route)]
    another operation x11 -> x0, other arithmetic: 13.8 us -> none  [transport(): return jnp.stack([rate_zero, rate_one, rate_two], axis)]
    add x10 -> x0, other arithmetic: 10.3 us -> none  [the longest x5 7.52 us: face_traces(): return (first + second + third, first - second + third)]
    another operation x4 -> x0, local copies, waits for them, and re-layouts: 8.23 us -> none  [the longest x2 6.92 us: face_traces(): second = jnp.take(field, 1, axis)]
    slice x15 -> x0, local copies, waits for them, and re-layouts: 6.61 us -> none  [the longest x2 2.16 us: block_rate(): jnp.roll(lower, -NZ, -1)]
    ppermute x4 -> x0, starting transfers between devices: 5.89 us -> none  [passed_along(): return lax.ppermute(block, axis, route)]
  transfers between devices with their start and end apart: 4 -> 0, of which waited for: 2 -> 0; matrix products, arithmetic and copies ran while one was open for 15% -> 0% of each run, Pallas kernels for 0% -> 0%
where the time goes in v1:
time: 70.8 us; the launch traced here: 70.6 us
  Pallas kernels  66.1 us (93%)
  local copies, waits for them, and re-layouts  4.45 us (6%)
    pallas_call x1, Pallas kernels, shards(): pl.pallas_call(functools.partial(kernel, nvel, nbox, count), out_shape=ja...  66.1 us
    unnamed x5, local copies, waits for them, and re-layouts  4.45 us

profile of v1, /device:TPU:0, one launch (start us, length us, event | category | flops | bytes accessed | tf_op | source)
XLA Modules:
  0.0 70.6 jit_solution(17082336664362225728)
XLA Ops:
  0.0 0.0 copy-start
  0.0 2.0 %copy-done = f32[256,3,3,3,1,128]{5,4,3,2,1,0:T(1,128)S(1)} copy-done((f32[256,3,3,3,1,128]{5,4,3,2,1,0:T(1,128)S(1)}, f32[256,3,3,3,1,128]{5,4,3,2,1,0:T(1,128)}, u32[]{:S(2)}) %copy-start) | copy-done | bytes 3538968
  2.0 0.0 copy-start.1
  2.0 0.7 copy-done.1
  2.7 66.1 %shard_map.28 = f32[6912,128]{1,0:T(8,128)S(1)} custom-call(f32[6912,128]{1,0:T(8,128)S(1)} %bitcast.3, f32[1,128]{1,0:T(1,128)S(1)} %copy-done.1), custom_call_target="tpu_custom_call" | custom-call | flops 70778880 | bytes 7077888 | tf_op jit(solution)/shard_map/pallas_call | solution.py:230
  68.8 1.8 %copy.6 = f32[256,3,3,3,1,128]{5,4,3,2,1,0:T(1,128)} copy(f32[256,3,3,3,1,128]{5,4,3,2,1,0:T(1,128)S(1)} %bitcast.2) | data formatting | bytes 7077888
Async XLA Ops:
  0.0 2.0 %copy-start = (f32[256,3,3,3,1,128]{5,4,3,2,1,0:T(1,128)S(1)}, f32[256,3,3,3,1,128]{5,4,3,2,1,0:T(1,128)}, u32[]{:S(2)}) copy-start(f32[256,3,3,3,1,128]{5,4,3,2,1,0:T(1,128)} %param.2) | copy-start | bytes 10616836
  2.0 0.7 copy-start.1

commit v2 on v1

--- a/solution.py
+++ b/solution.py
@@ -18,6 +18,7 @@
 FACE = MODES ** 2
 SUB = 8
 HALVES = VPD // SUB
+EARLY = 2
 MESH = pl.DeviceIdType.MESH
 
 
@@ -31,8 +32,8 @@
     return [first + a * stride for a in range(MODES)]
 
 
-def kernel(nvel, nbox, count, f_hbm, nu_ref, out_hbm, f_v, o_v, mid, trace, halo,
-           slots, in_sem, out_sem, x_send, x_recv, m_send, m_recv):
+def kernel(nvel, nbox, count, f_hbm, nu_ref, o_v, f_v, mid, trace, halo,
+           slots, in_sem, x_send, x_recv, m_send, m_recv):
     lanes = f_v.shape[-1]
     chunks = count // VPD
     rows = VPD * CUBE
@@ -50,14 +51,10 @@
         part = pl.ds(pl.multiple_of(c * rows, SUB), rows)
         return pltpu.make_async_copy(f_hbm.at[part], f_v.at[part], in_sem.at[c])
 
-    def store_copy(c):
-        part = pl.ds(pl.multiple_of(c * rows, SUB), rows)
-        return pltpu.make_async_copy(o_v.at[part], out_hbm.at[part], out_sem.at[c])
-
     def halo_copy(section, c):
+        s = section * chunks + c
         return pltpu.make_async_remote_copy(
-            src_ref=trace.at[section, c], dst_ref=halo.at[section, c],
-            send_sem=x_send.at[section, c], recv_sem=x_recv.at[section, c],
+            src_ref=trace.at[s], dst_ref=halo.at[s], send_sem=x_send.at[s], recv_sem=x_recv.at[s],
             device_id={"box": target}, device_id_type=MESH)
 
     def moment_copy(section, k, slot):
@@ -78,7 +75,6 @@
     pl.semaphore_signal(barrier, inc=1, device_id={"box": source}, device_id_type=MESH)
     each(1, nvel, lambda k: pl.semaphore_signal(
         barrier, inc=1, device_id={"vel": lax.rem(me_vel + k, nvel)}, device_id_type=MESH))
-    pl.semaphore_wait(barrier, nvel)
 
     speed_x = centre(first)
     sign_x = jnp.where(positive, 1.0, -1.0)
@@ -98,7 +94,7 @@
     def put_trace(section, c, h, values):
         for q in range(FACE):
             m0, m1, m2 = (values[m] for m in line_modes(0, q))
-            trace[section, c, h * FACE + q] = m0 + m2 + sign_x * m1
+            trace[section * chunks + c, h * FACE + q] = m0 + m2 + sign_x * m1
 
     def gathered(sums, c, h, base):
         speed_y = centre(lax.rem(start // VPD + c, VPD))
@@ -162,8 +158,8 @@
                   lambda q, i0, i1, i2: m[i0] + m[i2] + sign_y * m[i1],
                   lambda q, mine: pltpu.roll(mine, shift_y, 1))
         transport(0, speed_x, sign_x * speed_x,
-                  lambda q, i0, i1, i2: trace[section, c, h * FACE + q],
-                  lambda q, mine: halo[section, c, h * FACE + q])
+                  lambda q, i0, i1, i2: trace[section * chunks + c, h * FACE + q],
+                  lambda q, mine: halo[section * chunks + c, h * FACE + q])
         scale, flow_x, flow_y, flow_z, narrow = state
         off_x = speed_x - flow_x
         off_y = speed_y - flow_y
@@ -180,10 +176,18 @@
             values = field(c, h)
             put_trace(0, c, h, values)
             sums = gathered(sums, c, h, values[0])
+        return sums
+
+    def opening_sent(c, sums):
+        sums = opening(c, sums)
         halo_copy(0, c).start()
         return sums
 
-    exchange(0, lax.fori_loop(0, chunks, opening, zeros))
+    ready = min(EARLY, chunks)
+    sums = lax.fori_loop(0, ready, opening, zeros)
+    pl.semaphore_wait(barrier, nvel)
+    each(0, ready, lambda c: halo_copy(0, c).start())
+    exchange(0, lax.fori_loop(ready, chunks, opening_sent, sums))
     state_one = states(0)
 
     def section_one(c, sums):
@@ -209,14 +213,12 @@
             for m in range(CUBE):
                 place = pl.ds(base + m, SUB, stride=CUBE)
                 o_v[place, :] = 0.5 * f_v[place, :] + 0.5 * acc[m]
-        store_copy(c).start()
 
     each(0, chunks, section_two)
 
     for section in range(2):
         each(0, chunks, lambda c: halo_copy(section, c).wait_send())
         each(1, nvel, lambda k: moment_copy(section, k, me_vel).wait_send())
-    each(0, chunks, lambda c: store_copy(c).wait())
 
 
 def shards(nvel, nbox, distribution, collision_rate):
@@ -231,23 +233,21 @@
         functools.partial(kernel, nvel, nbox, count),
         out_shape=jax.ShapeDtypeStruct((total, lanes), f32),
         in_specs=[pl.BlockSpec(memory_space=pl.ANY), pl.BlockSpec(memory_space=pltpu.VMEM)],
-        out_specs=pl.BlockSpec(memory_space=pl.ANY),
+        out_specs=pl.BlockSpec(memory_space=pltpu.VMEM),
         scratch_shapes=[
             pltpu.VMEM((total, lanes), f32),
-            pltpu.VMEM((total, lanes), f32),
             pltpu.VMEM((chunks * HALVES, CUBE, SUB, lanes), f32),
-            pltpu.VMEM((2, chunks, HALVES * FACE, SUB, lanes), f32),
-            pltpu.VMEM((2, chunks, HALVES * FACE, SUB, lanes), f32),
+            pltpu.VMEM((2 * chunks, HALVES * FACE, SUB, lanes), f32),
+            pltpu.VMEM((2 * chunks, HALVES * FACE, SUB, lanes), f32),
             pltpu.VMEM((2, nvel, SUB, lanes), f32),
             pltpu.SemaphoreType.DMA((chunks,)),
-            pltpu.SemaphoreType.DMA((chunks,)),
-            pltpu.SemaphoreType.DMA((2, chunks)),
-            pltpu.SemaphoreType.DMA((2, chunks)),
+            pltpu.SemaphoreType.DMA((2 * chunks,)),
+            pltpu.SemaphoreType.DMA((2 * chunks,)),
             pltpu.SemaphoreType.DMA((2, nvel)),
             pltpu.SemaphoreType.DMA((2, nvel)),
         ],
         compiler_params=pltpu.CompilerParams(
-            collective_id=0, has_side_effects=True, vmem_limit_bytes=40 * 2 ** 20),
+            collective_id=0, has_side_effects=True, vmem_limit_bytes=50 * 2 ** 20),
         cost_estimate=pl.CostEstimate(flops=total * lanes * 80, bytes_accessed=total * lanes * 8,
                                       transcendentals=2 * count * lanes),
     )(distribution.reshape(total, lanes), collision_rate)

time: 70.8 us -> 63.6 us (0.90)
  Pallas kernels: 66.1 us -> 61 us
  local copies, waits for them, and re-layouts: 4.45 us -> 2.45 us
    pallas_call x1, Pallas kernels: 66.1 us -> 61 us  [shards(): pl.pallas_call(functools.partial(kernel, nvel, nbox, count), out_shape=ja...]
    unnamed x5 -> x3, local copies, waits for them, and re-layouts: 4.45 us -> 2.45 us
where the time goes in v2:
time: 63.6 us; the launch traced here: 63.4 us
  Pallas kernels  61 us (96%)
  local copies, waits for them, and re-layouts  2.45 us (4%)
    pallas_call x1, Pallas kernels, shards(): pl.pallas_call(functools.partial(kernel, nvel, nbox, count), out_shape=ja...  61 us
    unnamed x3, local copies, waits for them, and re-layouts  2.45 us

profile of v2, /device:TPU:0, one launch (start us, length us, event | category | flops | bytes accessed | tf_op | source)
XLA Modules:
  0.0 63.4 jit_solution(5661710563850381650)
XLA Ops:
  0.0 0.0 copy-start
  0.0 0.7 %copy-done = f32[1,128]{1,0:T(1,128)S(1)} copy-done((f32[1,128]{1,0:T(1,128)S(1)}, f32[1,128]{1,0:T(1,128)}, u32[]{:S(2)}) %copy-start) | copy-done | bytes 536
  0.7 61.0 %shard_map.28 = f32[6912,128]{1,0:T(8,128)S(1)} custom-call(f32[6912,128]{1,0:T(8,128)} %bitcast.3, f32[1,128]{1,0:T(1,128)S(1)} %copy-done), custom_call_target="tpu_custom_call" | custom-call | flops 70778880 | bytes 7077888 | tf_op jit(solution)/shard_map/pallas_call | solution.py:232
  61.6 1.8 %copy.6 = f32[256,3,3,3,1,128]{5,4,3,2,1,0:T(1,128)} copy(f32[256,3,3,3,1,128]{5,4,3,2,1,0:T(1,128)S(1)} %bitcast.2) | data formatting | bytes 7077888
Async XLA Ops:
  0.0 0.7 %copy-start = (f32[1,128]{1,0:T(1,128)S(1)}, f32[1,128]{1,0:T(1,128)}, u32[]{:S(2)}) copy-start(f32[1,128]{1,0:T(1,128)} %nu_ref.1) | copy-start | bytes 1540
